TPU v7x, 32 devices: a whole 2x2x4 slice. The times are simulated.
32 devices in a mesh: groups: 2 (over x), pair: 4 (over y, core), day: 4 (over z).
Axes of the slice: x: 2, y: 2, z: 4, core: 2. Of those that a mesh axis runs over, the one named last changes fastest.
Arguments:
- spectra: bfloat16 [8, 512, 4, 2048], P(('groups', 'day'), 'pair'), parts along dimension 0, may hold values from -6 to 6
- sub_pick: int32 [4, 2], P('day'), may hold values from 0 to 3, as said below
- pair_list: int32 [4, 2, 2], P('pair'), may hold values from 0 to 3, as said below
- slot_count: int32 [4], P('pair'), may hold values from 1 to 2
Outputs:
- stacks: float32 [16, 128, 8192], P(('groups', 'pair'), 'day'), parts along dimension 0
There are 2 independent parts, one for each index of `groups`. A program takes and returns all parts, laid end to end along the dimension named above; an argument that names none is the same for every part. Nothing has to cross between parts.
Inputs may be any that keep to these rules, and one draw needn't show every extreme that they name: `sub_pick`: in each row the 2 values are distinct. `pair_list`: for owner p every slot has a <= b <= a + 3 and p - 3 <= a, b <= p + 3.
All inputs are finite; a program needn't handle non-finite values.
Results may differ from a plain program's by a relative error of at most 0.0037.
Values may be sent and summed in bfloat16 or wider, within the bound.
A program may use at most 128 MiB of HBM per device.

v0:
```python
import jax
import jax.numpy as jnp
from jax import lax
from jax.sharding import PartitionSpec as P

LAGS = 64
REACH = 3


def passed_along(value, axis, by):
    count = lax.axis_size(axis)
    pairs = [(i, i + by) for i in range(count) if 0 <= i + by < count]
    return lax.ppermute(value, axis, pairs)


def lag_table(width, used):
    freq = jnp.arange(width, dtype=jnp.float32)[:, None]
    shift = (jnp.arange(LAGS) - LAGS // 2).astype(jnp.float32)[None, :]
    theta = jnp.pi * freq * shift / width
    scale = 1.0 / jnp.sqrt(jnp.float32(used * width))
    return jnp.concatenate([jnp.cos(theta) * scale, -jnp.sin(theta) * scale], 0).astype(
        jnp.bfloat16
    )


def correlate(left, right, table, width):
    channels = left.shape[0]
    row_block = 16
    right_real, right_imag = (right[..., :width], right[..., width:])

    def rows(piece):
        left_real, left_imag = (piece[..., :width], piece[..., width:])
        real = jnp.einsum("isf,jsf->ijf", left_real, right_real, preferred_element_type=jnp.float32)
        real = real + jnp.einsum(
            "isf,jsf->ijf", left_imag, right_imag, preferred_element_type=jnp.float32
        )
        imag = jnp.einsum("isf,jsf->ijf", left_real, right_imag, preferred_element_type=jnp.float32)
        imag = imag - jnp.einsum(
            "isf,jsf->ijf", left_imag, right_real, preferred_element_type=jnp.float32
        )
        cross = jnp.concatenate([real, imag], -1).astype(jnp.bfloat16)
        lagged = jnp.dot(
            cross.reshape(row_block * channels, 2 * width),
            table,
            preferred_element_type=jnp.float32,
        )
        return lagged.reshape(row_block, channels * table.shape[1])

    pieces = left.reshape(channels // row_block, row_block, left.shape[1], left.shape[2])
    return lax.map(rows, pieces).reshape(channels, channels * table.shape[1])


def per_device(spectra, sub_pick, pair_list, slot_count):
    local = spectra[0]
    picks = sub_pick[0]
    width = local.shape[2] // 2
    table = lag_table(width, picks.shape[0])
    here = lax.axis_index("pair")
    moved = jnp.take(local, picks, axis=1)
    nearby = []
    for step in range(-REACH, REACH + 1):
        if step == 0:
            nearby.append(moved)
        else:
            nearby.append(passed_along(moved, "pair", -step))
    pool = jnp.stack(nearby, 0)
    base = here - REACH
    pairs = pair_list[0]
    count = slot_count[0]

    def one_slot(pair):
        left = lax.dynamic_index_in_dim(pool, pair[0] - base, 0, keepdims=False)
        right = lax.dynamic_index_in_dim(pool, pair[1] - base, 0, keepdims=False)
        return correlate(left, right, table, width)

    lagged = lax.map(one_slot, pairs)
    alive = (jnp.arange(pairs.shape[0]) < count)[:, None, None]
    lagged = jnp.where(alive, lagged, jnp.zeros_like(lagged))
    return lax.psum_scatter(lagged, "day", scatter_dimension=1, tiled=True)


def solution(mesh):
    in_specs = (
        P(("groups", "day"), "pair", None, None),
        P("day", None),
        P("pair", None, None),
        P("pair"),
    )
    out_specs = P(("groups", "pair"), "day", None)
    return jax.shard_map(
        per_device, mesh=mesh, in_specs=in_specs, out_specs=out_specs, check_vma=False
    )
```

profile of v0, /device:TPU:11, one launch (start us, length us, event | category | flops | bytes accessed | tf_op | source)
XLA Modules:
  0.0 563.3 jit_solution(9181281400799410623)
XLA Ops:
  29.2 9.6 %collective-permute-done.1 = bf16[128,2,2048]{2,0,1:T(8,128)(2,1)} collective-permute-done((bf16[128,2,2048]{2,0,1:T(8,128)(2,1)S(1)}, bf16[128,2,2048]{2,0,1:T(8,128)(2,1)}, u32[]{:S(2)}, u32[]{:S(2)}) %collective-permute-start.1) | collective-permute-done | bytes 1048608 | tf_op jit(solution)/shard_map/ppermute | solution.py:13
  40.1 20.5 %collective-permute-done.2 = bf16[128,2,2048]{2,0,1:T(8,128)(2,1)} collective-permute-done((bf16[128,2,2048]{2,0,1:T(8,128)(2,1)S(1)}, bf16[128,2,2048]{2,0,1:T(8,128)(2,1)}, u32[]{:S(2)}, u32[]{:S(2)}) %collective-permute-start.2) | collective-permute-done | bytes 1048608 | tf_op jit(solution)/shard_map/ppermute | solution.py:13
  66.7 332.5 %while.24 = (s32[]{:T(128)}, f32[2,128,8192]{2,1,0:T(8,128)}, s32[2,2]{1,0:T(2,128)}, s32[]{:T(128)}, bf16[7,128,2,2048]{3,1,2,0:T(8,128)(2,1)}, /*index=5*/bf16...) while((s32[]{:T(128)}, f32[2,128,8192]{2,1,0:T(8,128)}, s32[2,2]{1,0:T(2,128)}, s32[]{:T(128)}, ...), condition=%wide.region_3.4_spmd.clone, body=%wide.region_0.3_spmd.sunk.clone | while | flops 595591168 | bytes 120325664 | solution.py:76
  73.4 155.0 %while.23 = (s32[]{:T(128)}, f32[8,16,8192]{2,1,0:T(8,128)}, bf16[8,16,2,2048]{3,1,0,2:T(8,128)(2,1)S(1)}, bf16[128,2,1024]{0,1,2:T(2,128)(2,1)}, bf16[128,2,102...) while((s32[]{:T(128)}, f32[8,16,8192]{2,1,0:T(8,128)}, bf16[8,16,2,2048]{3,1,0,2:T(8,128)(2,1)S(1)}, ...), condition=%wide.region_2.2_spmd, body=%wide.region_1.1_spmd.sunk | while | flops 595591168 | bytes 103547640 | solution.py:50
  84.4 4.5 copy_bitcast_fusion.4
  103.8 4.5 copy_bitcast_fusion.4
  123.2 4.5 copy_bitcast_fusion.4
  142.6 4.5 copy_bitcast_fusion.4
  161.9 4.5 copy_bitcast_fusion.4
  181.3 4.5 copy_bitcast_fusion.4
  200.7 4.5 copy_bitcast_fusion.4
  220.0 4.5 copy_bitcast_fusion.4
  228.4 4.5 bitcast_dynamic-update-slice_fusion.9
  239.6 155.0 %while.23 = (s32[]{:T(128)}, f32[8,16,8192]{2,1,0:T(8,128)}, bf16[8,16,2,2048]{3,1,0,2:T(8,128)(2,1)S(1)}, bf16[128,2,1024]{0,1,2:T(2,128)(2,1)}, bf16[128,2,102...) while((s32[]{:T(128)}, f32[8,16,8192]{2,1,0:T(8,128)}, bf16[8,16,2,2048]{3,1,0,2:T(8,128)(2,1)S(1)}, ...), condition=%wide.region_2.2_spmd, body=%wide.region_1.1_spmd.sunk | while | flops 595591168 | bytes 103547640 | solution.py:50
  250.7 4.5 copy_bitcast_fusion.4
  270.0 4.5 copy_bitcast_fusion.4
  308.8 4.5 copy_bitcast_fusion.4
  328.1 4.5 copy_bitcast_fusion.4
  347.5 4.5 copy_bitcast_fusion.4
  366.9 4.5 copy_bitcast_fusion.4
  386.2 4.5 copy_bitcast_fusion.4
  394.6 4.6 bitcast_dynamic-update-slice_fusion.9
  399.2 7.7 %broadcast_select_fusion = f32[2,128,8192]{2,1,0:T(8,128)} fusion(f32[2,128,8192]{2,1,0:T(8,128)} %get-tuple-element.69, pred[2]{0:T(512)(128)(4,1)S(1)} %copy-done.7), kind=kLoop, calls=%fused_computation.22 | loop fusion | flops 2097152 | bytes 16777218 | tf_op jit(solution)/shard_map/jit(_where)/select_n | solution.py:78
  406.9 149.6 %reduce-scatter.2.cloned.1.call-done = f32[2,32,8192]{2,1,0:T(8,128)} async-done(((f32[2,128,8192]{2,1,0:T(8,128)}), f32[2,32,8192]{2,1,0:T(8,128)}) %reduce-scatter.2.cloned.1.call-update) | async-done | bytes 2097168 | tf_op jit(solution)/shard_map/reduce_scatter | solution.py:79
  (385 shorter events, 281.7 us)
Async XLA Ops:
  6.5 549.9 %reduce-scatter.2.cloned.1.call-start = ((), (), s32[]{:S(2)}) async-start(), calls=%async_computation.1 | async-start | bytes 10485760 | tf_op jit(solution)/shard_map/reduce_scatter | solution.py:79
  11.4 15.8 %collective-permute-start = (bf16[128,2,2048]{2,0,1:T(8,128)(2,1)S(1)}, bf16[128,2,2048]{2,0,1:T(8,128)(2,1)}, u32[]{:S(2)}, u32[]{:S(2)}) collective-permute-start(bf16[128,2,2048]{2,0,1:T(8,128)(2,1)S(1)} %bitcast_select_fusion.1), channel_id=1, source_target_pairs={{0,12},{1,13},{2,14},{3,15},{16,28},{17,29},{18,30},{19,31}} | collective-permute-start | bytes 3145736 | tf_op jit(solution)/shard_map/ppermute | solution.py:13
  13.1 25.6 %collective-permute-start.1 = (bf16[128,2,2048]{2,0,1:T(8,128)(2,1)S(1)}, bf16[128,2,2048]{2,0,1:T(8,128)(2,1)}, u32[]{:S(2)}, u32[]{:S(2)}) collective-permute-start(bf16[128,2,2048]{2,0,1:T(8,128)(2,1)S(1)} %bitcast_select_fusion.1), channel_id=1, source_target_pairs={{0,8},{4,12},{1,9},{5,13},{2,10},{6,14},{3,11},{7,15},{16,24},{20,... | collective-permute-start | bytes 3145736 | tf_op jit(solution)/shard_map/ppermute | solution.py:13
  16.9 43.7 %collective-permute-start.2 = (bf16[128,2,2048]{2,0,1:T(8,128)(2,1)S(1)}, bf16[128,2,2048]{2,0,1:T(8,128)(2,1)}, u32[]{:S(2)}, u32[]{:S(2)}) collective-permute-start(bf16[128,2,2048]{2,0,1:T(8,128)(2,1)S(1)} %bitcast_select_fusion.1), channel_id=1, source_target_pairs={{0,4},{4,8},{8,12},{1,5},{5,9},{9,13},{2,6},{6,10},{10,14},{3,7},{... | collective-permute-start | bytes 3145736 | tf_op jit(solution)/shard_map/ppermute | solution.py:13
  18.8 43.4 %collective-permute-start.3 = (bf16[128,2,2048]{2,0,1:T(8,128)(2,1)S(1)}, bf16[128,2,2048]{2,0,1:T(8,128)(2,1)}, u32[]{:S(2)}, u32[]{:S(2)}) collective-permute-start(bf16[128,2,2048]{2,0,1:T(8,128)(2,1)S(1)} %bitcast_select_fusion.1), channel_id=1, source_target_pairs={{4,0},{8,4},{12,8},{5,1},{9,5},{13,9},{6,2},{10,6},{14,10},{7,3},{... | collective-permute-start | bytes 3145736 | tf_op jit(solution)/shard_map/ppermute | solution.py:13
  22.5 41.0 %collective-permute-start.4 = (bf16[128,2,2048]{2,0,1:T(8,128)(2,1)S(1)}, bf16[128,2,2048]{2,0,1:T(8,128)(2,1)S(1)}, u32[]{:S(2)}, u32[]{:S(2)}) collective-permute-start(bf16[128,2,2048]{2,0,1:T(8,128)(2,1)S(1)} %bitcast_select_fusion.1), channel_id=1, source_target_pairs={{8,0},{12,4},{9,1},{13,5},{10,2},{14,6},{11,3},{15,7},{24,16},{28,... | collective-permute-start | bytes 3145736 | tf_op jit(solution)/shard_map/ppermute | solution.py:13
  27.2 36.4 %collective-permute-start.5 = (bf16[128,2,2048]{2,0,1:T(8,128)(2,1)S(1)}, bf16[128,2,2048]{2,0,1:T(8,128)(2,1)S(1)}, u32[]{:S(2)}, u32[]{:S(2)}) collective-permute-start(bf16[128,2,2048]{2,0,1:T(8,128)(2,1)S(1)} %bitcast_select_fusion.1), channel_id=1, source_target_pairs={{12,0},{13,1},{14,2},{15,3},{28,16},{29,17},{30,18},{31,19}} | collective-permute-start | bytes 3145736 | tf_op jit(solution)/shard_map/ppermute | solution.py:13
  66.7 332.5 %copy-start.7 = (pred[2]{0:T(512)(128)(4,1)S(1)}, pred[2]{0:T(512)(128)(4,1)}, u32[]{:S(2)}) copy-start(pred[2]{0:T(512)(128)(4,1)} %iota_compare_fusion) | copy-start | bytes 10
  84.4 4.5 copy-start.6
  103.8 4.5 copy-start.6
  123.2 4.5 copy-start.6
  142.6 4.5 copy-start.6
  161.9 4.5 copy-start.6
  181.3 4.5 copy-start.6
  200.7 4.5 copy-start.6
  220.0 4.5 copy-start.6
  250.6 4.5 copy-start.6
  270.0 4.5 copy-start.6
  289.4 4.5 copy-start.6
  308.8 4.5 copy-start.6
  328.1 4.5 copy-start.6
  347.5 4.5 copy-start.6
  366.9 4.5 copy-start.6
  386.2 4.5 copy-start.6
  (81 other events, 217.5 us)
Sparse Core Ops, SparseCore 0:
  407.0 149.4 reduce-scatter.1
where the time goes:
time: 567 us; the launch traced here: 563 us
  matrix products  205 us (36%)
  waiting for transfers between devices  180 us (32%)
  local copies, waits for them, and re-layouts  136 us (24%)
  between operations  14.2 us (3%)
  starting transfers between devices  13.1 us (2%)
  other arithmetic  11.2 us (2%)
    reduce_scatter x1, waiting for transfers between devices, per_device(): return lax.psum_scatter(lagged, 'day', scatter_dimension=1, tiled=True)  150 us
    concatenate x16, local copies, waits for them, and re-layouts, rows(): cross = jnp.concatenate([real, imag], -1).astype(jnp.bfloat16)  71.4 us
    dot_general x16, matrix products, rows(): jnp.einsum('isf,jsf->ijf', left_imag, right_imag, preferred_element_type=...  64.5 us
    dot_general x16, matrix products, rows(): jnp.dot(cross.reshape(row_block * channels, 2 * width), table, preferred_...  42.1 us
    dot_general x16, matrix products, rows(): jnp.einsum('isf,jsf->ijf', left_real, right_real, preferred_element_type=...  40.9 us
    dot_general x16, matrix products, rows(): jnp.einsum('isf,jsf->ijf', left_imag, right_real, preferred_element_type=...  34 us
    ppermute x6, waiting for transfers between devices, passed_along(): return lax.ppermute(value, axis, pairs)  30.1 us
    dot_general x16, matrix products, rows(): jnp.einsum('isf,jsf->ijf', left_real, right_imag, preferred_element_type=...  23.3 us
  transfers between devices with their start and end apart: 7, of which 3 were waited for; matrix products, arithmetic and copies ran while one was open for 1% of the time, Pallas kernels for 0%

commit v1 on v0

v1 whole, which is shorter than its diff:
```python
import functools

import jax
import jax.numpy as jnp
import numpy as np
from jax import lax
from jax.experimental import pallas as pl
from jax.experimental.pallas import tpu as pltpu
from jax.sharding import PartitionSpec as P

LAGS = 64
HALF = LAGS // 2
REACH = 3
GROUP = 8
CHUNK = 256
MESH = pl.DeviceIdType.MESH


def lag_rows(width, used):
    freq = np.arange(width, dtype=np.float32)[None, :]
    shift = np.arange(HALF, dtype=np.float32)[:, None]
    shift_sin = shift.copy()
    shift_sin[0, 0] = -HALF
    scale = np.float32(1.0) / np.sqrt(np.float32(used * width))
    turn = np.float32(np.pi)
    cosine = np.cos(turn * freq * shift / np.float32(width)) * scale
    sine = -np.sin(turn * freq * shift_sin / np.float32(width)) * scale
    edge = np.zeros((16, width), np.float32)
    edge[0] = np.cos(turn * freq[0] * np.float32(-HALF) / np.float32(width)) * scale
    return jnp.asarray(np.concatenate([cosine, sine, edge], 0), jnp.bfloat16)


def lag_block(left_ref, right_ref, rows_ref, slot, row, width, used):
    chunks = width // CHUNK
    total = None
    piece = left_ref[slot, pl.ds(pl.multiple_of(row, GROUP), GROUP), :]
    for sub in range(used):
        for c in range(chunks):
            at = slice(c * CHUNK, (c + 1) * CHUNK)
            cos = rows_ref[0:HALF, at]
            sin_low = rows_ref[HALF : HALF + 16, at]
            sin_high = rows_ref[HALF + 16 : 2 * HALF, at]
            edge = rows_ref[2 * HALF : 2 * HALF + 16, at]
            start = sub * 2 * width + c * CHUNK
            real = piece[:, start : start + CHUNK]
            imag = piece[:, start + width : start + width + CHUNK]
            built = []
            for i in range(GROUP):
                re = jnp.broadcast_to(real[i : i + 1], (16, CHUNK)).astype(jnp.bfloat16)
                im = jnp.broadcast_to(imag[i : i + 1], (16, CHUNK)).astype(jnp.bfloat16)
                with_real = [
                    re * cos[:16], re * cos[16:], re * edge - im * sin_low, -(im * sin_high)
                ]
                with_imag = [
                    im * cos[:16], im * cos[16:], im * edge + re * sin_low, re * sin_high
                ]
                built.append(
                    jnp.concatenate(
                        [jnp.concatenate(with_real, 0), jnp.concatenate(with_imag, 0)], 1
                    )
                )
            weights = jnp.concatenate(built, 0)
            depth = (sub * chunks + c) * 2 * CHUNK
            part = jnp.dot(
                weights,
                right_ref[slot, depth : depth + 2 * CHUNK, :],
                preferred_element_type=jnp.float32,
            )
            total = part if total is None else total + part
    return total


def stack_kernel(
    days, width, used, left_ref, right_ref, rows_ref, out_ref, send, recv, send_sem, recv_sem
):
    slots, channels = left_ref.shape[0], left_ref.shape[1]
    share = channels // days
    steps = share // GROUP
    high = GROUP * LAGS
    me = lax.axis_index("day")

    barrier = pltpu.get_barrier_semaphore()
    for by in range(1, days):
        pl.semaphore_signal(
            barrier, inc=1, device_id={"day": lax.rem(me + by, days)}, device_id_type=MESH
        )

    def transfer(n):
        by = n // slots + 1
        return pltpu.make_async_remote_copy(
            src_ref=send.at[n],
            dst_ref=recv.at[n],
            send_sem=send_sem.at[n],
            recv_sem=recv_sem.at[n],
            device_id={"day": lax.rem(me + by, days)},
            device_id_type=MESH,
        )

    def block(slot, owner, step):
        return lag_block(
            left_ref, right_ref, rows_ref, slot, owner * share + step * GROUP, width, used
        )

    def send_piece(n, carry):
        owner = lax.rem(me + n // slots + 1, days)
        slot = lax.rem(n, slots)

        def one(step, inner):
            at = pl.ds(pl.multiple_of(step * high, high), high)
            send[n, at, :] = block(slot, owner, step).astype(jnp.bfloat16)
            return inner

        lax.fori_loop(0, steps, one, 0)

        @pl.when(n == 0)
        def _():
            pl.semaphore_wait(barrier, days - 1)

        transfer(n).start()
        return carry

    lax.fori_loop(0, (days - 1) * slots, send_piece, 0)

    def own_piece(n, carry):
        slot, step = n // steps, lax.rem(n, steps)
        at = pl.ds(pl.multiple_of(step * high, high), high)
        out_ref[slot, at, :] = block(slot, me, step)
        return carry

    lax.fori_loop(0, slots * steps, own_piece, 0)

    def add_piece(n, carry):
        slot = lax.rem(n, slots)
        transfer(n).wait()
        out_ref[slot] = out_ref[slot] + recv[n].astype(jnp.float32)
        return carry

    lax.fori_loop(0, (days - 1) * slots, add_piece, 0)


def stacked(left, right, rows, days, width, used):
    slots, channels = left.shape[0], left.shape[1]
    tall = channels // days * LAGS
    copies = (days - 1) * slots
    cost = 2 * slots * channels * LAGS * left.shape[2] * channels
    return pl.pallas_call(
        functools.partial(stack_kernel, days, width, used),
        out_shape=jax.ShapeDtypeStruct((slots, tall, channels), jnp.float32),
        in_specs=[pl.BlockSpec(memory_space=pltpu.VMEM)] * 3,
        out_specs=pl.BlockSpec(memory_space=pltpu.VMEM),
        scratch_shapes=[
            pltpu.VMEM((copies, tall, channels), jnp.bfloat16),
            pltpu.VMEM((copies, tall, channels), jnp.bfloat16),
            pltpu.SemaphoreType.DMA((copies,)),
            pltpu.SemaphoreType.DMA((copies,)),
        ],
        compiler_params=pltpu.CompilerParams(
            collective_id=0, has_side_effects=True, vmem_limit_bytes=48 * 1024 * 1024
        ),
        cost_estimate=pl.CostEstimate(flops=cost, bytes_accessed=1 << 23, transcendentals=0),
    )(left, right, rows)


def passed_along(value, by):
    count = lax.axis_size("pair")
    pairs = [(i, i + by) for i in range(count) if 0 <= i + by < count]
    return lax.ppermute(value, "pair", pairs)


def swapped(value, mask):
    count = lax.axis_size("pair")
    return lax.ppermute(value, "pair", [(i, i ^ mask) for i in range(count)])


def gathered(moved, wanted):
    here = lax.axis_index("pair")
    if lax.axis_size("pair") == 4:
        far = swapped(moved, 2)
        pool = jnp.stack([moved, swapped(moved, 1), far, swapped(far, 1)], 0)
        return pool, wanted ^ here
    nearby = [
        moved if step == 0 else passed_along(moved, -step) for step in range(-REACH, REACH + 1)
    ]
    return jnp.stack(nearby, 0), wanted - (here - REACH)


def per_device(spectra, sub_pick, pair_list, slot_count):
    local = spectra[0]
    picks = sub_pick[0]
    channels, width, used = local.shape[0], local.shape[2] // 2, picks.shape[0]
    days = lax.axis_size("day")
    moved = jnp.take(local, picks, axis=1).reshape(channels, used * 2 * width)
    pairs = pair_list[0]
    slots = pairs.shape[0]
    pool, place = gathered(moved, pairs)
    left = jnp.take(pool, place[:, 0], axis=0).astype(jnp.float32)
    right = jnp.take(pool, place[:, 1], axis=0)
    right = right.reshape(slots, channels, used, 2, width // CHUNK, CHUNK)
    right = right.transpose(0, 2, 4, 3, 5, 1).reshape(slots, used * 2 * width, channels)

    summed = stacked(left, right, lag_rows(width, used), days, width, used)
    summed = summed.reshape(slots, channels // days, LAGS, channels)
    even, odd = summed[:, :, :HALF], summed[:, :, HALF:]
    ahead = even[:, :, 1:] + odd[:, :, 1:]
    behind = even[:, :, 1:] - odd[:, :, 1:]
    lagged = jnp.concatenate([odd[:, :, :1], behind[:, :, ::-1], even[:, :, :1], ahead], 2)
    alive = (jnp.arange(slots) < slot_count[0])[:, None, None, None]
    lagged = jnp.where(alive, lagged, jnp.zeros_like(lagged))
    return lagged.transpose(0, 1, 3, 2).reshape(slots, channels // days, channels * LAGS)


def solution(mesh):
    in_specs = (
        P(("groups", "day"), "pair", None, None),
        P("day", None),
        P("pair", None, None),
        P("pair"),
    )
    out_specs = P(("groups", "pair"), "day", None)
    return jax.shard_map(
        per_device, mesh=mesh, in_specs=in_specs, out_specs=out_specs, check_vma=False
    )
```

time: 567 us -> 229 us (0.40)
  matrix products: 205 us -> 0 us
  waiting for transfers between devices: 180 us -> 22.9 us
  Pallas kernels: 0 us -> 101 us
  local copies, waits for them, and re-layouts: 136 us -> 68 us
  other arithmetic: 11.2 us -> 29.9 us
  between operations: 14.2 us -> 0.81 us
  starting transfers between devices: 13.1 us -> 3.81 us
    dot_general x80 -> x0, matrix products: 205 us -> none  [the longest x16 64.5 us: rows(): jnp.einsum('isf,jsf->ijf', left_imag, right_imag, preferred_element_type=...]
    reduce_scatter x1 -> x0, waiting for transfers between devices: 150 us -> none  [per_device(): return lax.psum_scatter(lagged, 'day', scatter_dimension=1, tiled=True)]
    pallas_call x0 -> x1, Pallas kernels: none -> 101 us  [stacked(): pl.pallas_call(functools.partial(stack_kernel, days, width, used), out_sh...]
    concatenate x16 -> x0, local copies, waits for them, and re-layouts: 71.4 us -> none  [rows(): cross = jnp.concatenate([real, imag], -1).astype(jnp.bfloat16)]
    rev x0 -> x1, local copies, waits for them, and re-layouts: none -> 34 us  [per_device(): behind[:, :, ::-1]]
    dynamic_update_slice x18 -> x0, local copies, waits for them, and re-layouts: 22.5 us -> none  [the longest x16 13.4 us: correlate(): return lax.map(rows, pieces).reshape(channels, channels * table.shape[1])]
    dynamic_slice x38 -> x0, local copies, waits for them, and re-layouts: 18.2 us -> none  [the longest x32 11.9 us: correlate(): return lax.map(rows, pieces).reshape(channels, channels * table.shape[1])]
    transpose x0 -> x1, other arithmetic: none -> 11.1 us  [per_device(): lagged.transpose(0, 1, 3, 2)]
  transfers between devices with their start and end apart: 7 -> 3, of which waited for: 3 -> 2; matrix products, arithmetic and copies ran while one was open for 1% -> 0% of each run, Pallas kernels for 0% -> 0%
where the time goes in v1:
time: 229 us; the launch traced here: 226 us
  Pallas kernels  101 us (44%)
  local copies, waits for them, and re-layouts  68 us (30%)
  other arithmetic  29.9 us (13%)
  waiting for transfers between devices  22.9 us (10%)
  starting transfers between devices  3.81 us (2%)
    pallas_call x1, Pallas kernels, stacked(): pl.pallas_call(functools.partial(stack_kernel, days, width, used), out_sh...  101 us
    rev x1, local copies, waits for them, and re-layouts, per_device(): behind[:, :, ::-1]  34 us
    ppermute x3, waiting for transfers between devices, swapped(): return lax.ppermute(value, 'pair', [(i, i ^ mask) for i in range(count)])  22.9 us
    unnamed x9, local copies, waits for them, and re-layouts  13.3 us
    transpose x1, other arithmetic, per_device(): lagged.transpose(0, 1, 3, 2)  11.1 us
    sub x1, other arithmetic, per_device(): behind = even[:, :, 1:] - odd[:, :, 1:]  8.33 us
    reshape x1, local copies, waits for them, and re-layouts, per_device(): lagged.transpose(0, 1, 3, 2)  4.76 us
  transfers between devices with their start and end apart: 3, of which 2 were waited for; matrix products, arithmetic and copies ran while one was open for 0% of the time, Pallas kernels for 0%

profile of v1, /device:TPU:11, one launch (start us, length us, event | category | flops | bytes accessed | tf_op | source)
XLA Modules:
  0.0 226.2 jit_solution(7638703684465477873)
XLA Ops:
  0.7 0.7 compare_and_fusion.2
  1.4 2.7 %copy.29 = bf16[1,128,4,2048]{3,1,2,0:T(8,128)(2,1)S(1)} copy(bf16[1,128,4,2048]{3,2,1,0:T(4,128)(2,1)} %param.7) | data formatting | bytes 4194304 | tf_op args[0]
  4.8 0.7 copy.14
  6.1 1.3 collective-permute-start.1
  7.4 1.0 collective-permute-start
  9.9 20.5 %collective-permute-done.1 = bf16[128,4096]{1,0:T(8,128)(2,1)} collective-permute-done((bf16[128,4096]{1,0:T(8,128)(2,1)S(1)}, bf16[128,4096]{1,0:T(8,128)(2,1)}, u32[]{:S(2)}, u32[]{:S(2)}) %collective-permute-start.1) | collective-permute-done | bytes 1048608 | tf_op jit(solution)/shard_map/ppermute | solution.py:172
  30.3 1.5 collective-permute-start.2
  32.0 2.4 %collective-permute-done.2 = bf16[128,4096]{1,0:T(8,128)(2,1)S(1)} collective-permute-done((bf16[128,4096]{1,0:T(8,128)(2,1)}, bf16[128,4096]{1,0:T(8,128)(2,1)S(1)}, u32[]{:S(2)}, u32[]{:S(2)}) %collective-permute-start.2) | collective-permute-done | bytes 1048608 | tf_op jit(solution)/shard_map/ppermute | solution.py:172
  34.4 3.4 %pad_maximum_fusion = bf16[4,128,4096]{2,1,0:T(8,128)(2,1)} fusion(bf16[1,128,4096]{2,1,0:T(8,128)(2,1)S(1)} %bitcast.36, bf16[1,128,4096]{2,1,0:T(8,128)(2,1)} %bitcast.10, bf16[1,128,4096]{2,1,0:T(8,128)(2,1)} %bitcast.9, bf16[1,128,4096]{2,1,0:T(8,128)(2,1)S(1)} %broadcast_select_fusion.2), kind=kLoop, calls=%fused_computation.3 | loop fusion | flops 6291456 | bytes 8388608 | tf_op jit(solution)/shard_map/stack | solution.py:179
  37.8 4.2 %gather_fusion.2 = bf16[2,128,4096]{2,1,0:T(8,128)(2,1)} fusion(bf16[4,128,4096]{2,1,0:T(8,128)(2,1)} %pad_maximum_fusion, s32[1024]{0:T(1024)S(1)} %pad_clamp_fusion), kind=kCustom, calls=%fused_computation.1.clone | custom fusion | bytes 4194312 | tf_op jit(solution)/shard_map/jit(_take)/gather | solution.py:197
  42.0 2.9 %gather_fusion.1 = bf16[2,128,4096]{2,1,0:T(8,128)(2,1)S(1)} fusion(bf16[4,128,4096]{2,1,0:T(8,128)(2,1)} %pad_maximum_fusion, s32[1024]{0:T(1024)S(1)} %pad_clamp_fusion.1), kind=kCustom, calls=%fused_computation.clone | custom fusion | bytes 4194312 | tf_op jit(solution)/shard_map/jit(_take)/gather | solution.py:196
  44.9 3.2 %broadcast_select_fusion = bf16[2,128,4096]{2,1,0:T(8,128)(2,1)} fusion(bf16[2,128,4096]{2,1,0:T(8,128)(2,1)} %gather_fusion.2, pred[2]{0:T(512)(128)(4,1)S(1)} %get-tuple-element.16), kind=kLoop, calls=%fused_computation.8 | loop fusion | flops 1048576 | bytes 4194306 | tf_op jit(solution)/shard_map/jit(_take)/select_n | solution.py:197
  48.0 4.1 %copy.18 = bf16[2,128,4096]{1,2,0:T(8,128)(2,1)} copy(bf16[2,128,4096]{2,1,0:T(8,128)(2,1)} %broadcast_select_fusion) | data formatting | bytes 4194304 | tf_op jit(solution)/shard_map/jit(_take)/select_n | solution.py:197
  52.1 1.8 copy.19
  53.9 2.3 %select_convert_fusion.left_ref = f32[2,128,4096]{2,1,0:T(8,128)} fusion(bf16[2,128,4096]{2,1,0:T(8,128)(2,1)S(1)} %gather_fusion.1, pred[2]{0:T(512)(128)(4,1)S(1)} %get-tuple-element.17), kind=kLoop, calls=%fused_computation.7 | loop fusion | flops 2097152 | bytes 6291458 | tf_op jit(solution)/shard_map/convert_element_type | solution.py:196
  56.2 100.8 %shard_map.55 = f32[2,2048,128]{2,1,0:T(8,128)S(1)} custom-call(f32[2,128,4096]{2,1,0:T(8,128)} %select_convert_fusion.left_ref, bf16[2,4096,128]{2,1,0:T(8,128)(2,1)S(1)} %bitcast.30, bf16[80,1024]{1,0:T(8,128)(2,1)S(1)} %copy-done), custom_call_target="tpu_custom_call" | custom-call | flops 17179869184 | bytes 8388608 | tf_op jit(solution)/shard_map/pallas_call | solution.py:146
  157.4 2.7 %copy.26 = f32[2,32,31,128]{2,3,1,0:T(8,128)} copy(f32[2,32,31,128]{3,2,1,0:T(8,128)S(1)} %get-tuple-element.12) | data formatting | bytes 2031616
  160.1 2.6 %copy.24 = f32[2,32,1,128]{2,3,1,0:T(8,128)} copy(f32[2,32,1,128]{3,2,1,0:T(1,128)S(1)} %get-tuple-element.10) | data formatting | bytes 65536
  162.7 2.7 %copy.25 = f32[2,32,31,128]{2,3,1,0:T(8,128)} copy(f32[2,32,31,128]{3,2,1,0:T(8,128)S(1)} %get-tuple-element.13) | data formatting | bytes 2031616
  165.4 8.3 %fusion.2 = (f32[2,32,31,128]{2,3,1,0:T(8,128)}, f32[2,32,31,128]{2,3,1,0:T(8,128)}) fusion(f32[2,32,31,128]{2,3,1,0:T(8,128)} %copy.25, f32[2,32,31,128]{2,3,1,0:T(8,128)} %copy.26), kind=kLoop, calls=%fused_computation.26 | loop fusion | flops 507904 | bytes 4063232 | tf_op jit(solution)/shard_map/sub | solution.py:205
  173.7 34.0 %rev.3 = f32[2,32,31,128]{2,3,1,0:T(8,128)} reverse(f32[2,32,31,128]{2,3,1,0:T(8,128)} %get-tuple-element.8), dimensions={2} | reverse | bytes 2031616 | tf_op jit(solution)/shard_map/rev | solution.py:206
  207.7 2.6 %copy.27 = f32[2,32,1,128]{2,3,1,0:T(8,128)} copy(f32[2,32,1,128]{3,2,1,0:T(1,128)S(1)} %get-tuple-element.11) | data formatting | bytes 65536
  210.3 11.1 %fusion = f32[2,32,128,64]{3,2,1,0:T(8,128)} fusion(f32[2,32,31,128]{2,3,1,0:T(8,128)} %get-tuple-element.9, f32[2,32,1,128]{2,3,1,0:T(8,128)} %copy.27, f32[2,32,31,128]{2,3,1,0:T(8,128)} %rev.3, f32[2,32,1,128]{2,3,1,0:T(8,128)} %copy.24, pred[2]{0:T(512)(128)(4,1)S(1)} %iota_compare_fusion), kind=kLoop, calls=%fused_computation.5 | loop fusion | flops 2097152 | bytes 4194306 | tf_op jit(solution)/shard_map/transpose | solution.py:209
  221.4 4.8 %reshape.92 = f32[2,32,8192]{2,1,0:T(8,128)} reshape(f32[2,32,128,64]{3,2,1,0:T(8,128)} %fusion) | data formatting | bytes 4194304 | tf_op jit(solution)/shard_map/reshape | solution.py:209
  (23 shorter events, 3.3 us)
Async XLA Ops:
  4.8 4.8 %copy-start.1 = (s32[1,2,2]{2,1,0:T(2,128)S(1)}, s32[1,2,2]{2,1,0:T(2,128)}, u32[]{:S(2)}) copy-start(s32[1,2,2]{2,1,0:T(2,128)} %param.9) | copy-start | bytes 52
  6.1 24.2 %collective-permute-start.1 = (bf16[128,4096]{1,0:T(8,128)(2,1)S(1)}, bf16[128,4096]{1,0:T(8,128)(2,1)}, u32[]{:S(2)}, u32[]{:S(2)}) collective-permute-start(bf16[128,4096]{1,0:T(8,128)(2,1)S(1)} %broadcast_select_fusion.1), channel_id=1, source_target_pairs={{0,8},{4,12},{8,0},{12,4},{1,9},{5,13},{9,1},{13,5},{2,10},{6,14},... | collective-permute-start | bytes 3145736 | tf_op jit(solution)/shard_map/ppermute | solution.py:172
  7.4 24.6 %collective-permute-start = (bf16[128,4096]{1,0:T(8,128)(2,1)S(1)}, bf16[128,4096]{1,0:T(8,128)(2,1)}, u32[]{:S(2)}, u32[]{:S(2)}) collective-permute-start(bf16[128,4096]{1,0:T(8,128)(2,1)S(1)} %broadcast_select_fusion.1), channel_id=1, source_target_pairs={{0,4},{4,0},{8,12},{12,8},{1,5},{5,1},{9,13},{13,9},{2,6},{6,2},{1... | collective-permute-start | bytes 3145736 | tf_op jit(solution)/shard_map/ppermute | solution.py:172
  30.3 4.0 %collective-permute-start.2 = (bf16[128,4096]{1,0:T(8,128)(2,1)}, bf16[128,4096]{1,0:T(8,128)(2,1)S(1)}, u32[]{:S(2)}, u32[]{:S(2)}) collective-permute-start(bf16[128,4096]{1,0:T(8,128)(2,1)} %collective-permute-done.1), channel_id=1, source_target_pairs={{0,4},{4,0},{8,12},{12,8},{1,5},{5,1},{9,13},{13,9},{2,6},{6,2},{1... | collective-permute-start | bytes 3145736 | tf_op jit(solution)/shard_map/ppermute | solution.py:172
  53.9 2.3 %copy-start = (bf16[80,1024]{1,0:T(8,128)(2,1)S(1)}, bf16[80,1024]{1,0:T(8,128)(2,1)}, u32[]{:S(2)}) copy-start(bf16[80,1024]{1,0:T(8,128)(2,1)} %constant.35.clone.rows_ref) | copy-start | bytes 491524

commit v2 on v1

--- a/solution.py
+++ b/solution.py
@@ -70,14 +70,37 @@
     return total
 
 
+def laid_out(days, me):
+    if days != 4:
+        return lambda k: (lax.rem(me + k + 1, days), lax.rem(me + k + 1, days), k, k < 0)
+    inner = lax.rem((me + 1) // 2, 2)
+    low = 1 - me // 2
+
+    def piece(k):
+        outer_owner = low * (3 - k) + (1 - low) * k
+        inner_first = low * 0 + (1 - low) * 3
+        inner_owner = low * (4 - k) + (1 - low) * (k - 1)
+        first = 1 - jnp.minimum(k, 1)
+        inner_owner = first * inner_first + (1 - first) * inner_owner
+        owner = inner * inner_owner + (1 - inner) * outer_owner
+        target = inner * inner_owner + (1 - inner) * (low * 1 + (1 - low) * 2)
+        landing = inner * (3 - first) + (1 - inner) * k
+        return owner, target, landing, jnp.logical_and(inner == 1, k >= 1)
+
+    return piece
+
+
 def stack_kernel(
-    days, width, used, left_ref, right_ref, rows_ref, out_ref, send, recv, send_sem, recv_sem
+    days, width, used, left_ref, right_ref, rows_ref, out_ref,
+    send, recv, own, fresh, turned, flat, send_sem, recv_sem,
 ):
     slots, channels = left_ref.shape[0], left_ref.shape[1]
     share = channels // days
     steps = share // GROUP
     high = GROUP * LAGS
     me = lax.axis_index("day")
+    piece = laid_out(days, me)
+    finals = (2, 3) if days == 4 else tuple(range(days - 1))
 
     barrier = pltpu.get_barrier_semaphore()
     for by in range(1, days):
@@ -85,16 +108,18 @@
             barrier, inc=1, device_id={"day": lax.rem(me + by, days)}, device_id_type=MESH
         )
 
-    def transfer(n):
-        by = n // slots + 1
+    def transfer(n, slot, target, landing):
         return pltpu.make_async_remote_copy(
             src_ref=send.at[n],
-            dst_ref=recv.at[n],
+            dst_ref=recv.at[landing, slot],
             send_sem=send_sem.at[n],
-            recv_sem=recv_sem.at[n],
-            device_id={"day": lax.rem(me + by, days)},
+            recv_sem=recv_sem.at[landing, slot],
+            device_id={"day": target},
             device_id_type=MESH,
         )
+
+    def span(step):
+        return pl.ds(pl.multiple_of(step * high, high), high)
 
     def block(slot, owner, step):
         return lag_block(
@@ -102,57 +127,115 @@
         )
 
     def send_piece(n, carry):
-        owner = lax.rem(me + n // slots + 1, days)
-        slot = lax.rem(n, slots)
+        k, slot = n // slots, lax.rem(n, slots)
+        owner, target, landing, adds = piece(k)
 
         def one(step, inner):
-            at = pl.ds(pl.multiple_of(step * high, high), high)
-            send[n, at, :] = block(slot, owner, step).astype(jnp.bfloat16)
+            fresh[span(step), :] = block(slot, owner, step)
             return inner
 
         lax.fori_loop(0, steps, one, 0)
+
+        if days == 4:
+            @pl.when(adds)
+            def _():
+                transfer(n, slot, target, k - 1).wait_recv()
+                send[n] = (fresh[...] + recv[k - 1, slot].astype(jnp.float32)).astype(jnp.bfloat16)
+
+            @pl.when(jnp.logical_not(adds))
+            def _():
+                send[n] = fresh[...].astype(jnp.bfloat16)
+        else:
+            send[n] = fresh[...].astype(jnp.bfloat16)
 
         @pl.when(n == 0)
         def _():
             pl.semaphore_wait(barrier, days - 1)
 
-        transfer(n).start()
+        transfer(n, slot, target, landing).start()
         return carry
 
     lax.fori_loop(0, (days - 1) * slots, send_piece, 0)
 
     def own_piece(n, carry):
         slot, step = n // steps, lax.rem(n, steps)
-        at = pl.ds(pl.multiple_of(step * high, high), high)
-        out_ref[slot, at, :] = block(slot, me, step)
+        own[slot, span(step), :] = block(slot, me, step)
         return carry
 
     lax.fori_loop(0, slots * steps, own_piece, 0)
 
-    def add_piece(n, carry):
-        slot = lax.rem(n, slots)
-        transfer(n).wait()
-        out_ref[slot] = out_ref[slot] + recv[n].astype(jnp.float32)
-        return carry
-
-    lax.fori_loop(0, (days - 1) * slots, add_piece, 0)
+    lane = lax.broadcasted_iota(jnp.int32, (LAGS, 2 * LAGS), 1)
+    lag = lane % LAGS
+    away = jnp.abs(lag - HALF)
+    half = lane - lag
+    even_at = half + away
+    odd_at = half + HALF + jnp.minimum(away, HALF - 1)
+    sign = jnp.where(lag > HALF, 1.0, jnp.where((lag > 0) & (lag < HALF), -1.0, 0.0))
+
+    def joined(x):
+        even = jnp.take_along_axis(x, even_at, axis=1)
+        odd = jnp.take_along_axis(x, odd_at, axis=1)
+        return even + sign * odd
+
+    def finish(n, carry):
+        slot, step = n // steps, lax.rem(n, steps)
+
+        @pl.when(step == 0)
+        def _():
+            for f in finals:
+                transfer(0, slot, lax.rem(me + 1, days), f).wait_recv()
+
+        total = own[slot, span(step), :]
+        for f in finals:
+            total = total + recv[f, slot, span(step), :].astype(jnp.float32)
+        for q in range(GROUP // 2):
+            turned[q] = total[q * 2 * LAGS : (q + 1) * 2 * LAGS].T
+        for q in range(GROUP // 2):
+            first = turned[q, pl.ds(0, LAGS, stride=2), :]
+            second = turned[q, pl.ds(1, LAGS, stride=2), :]
+            flat[2 * q * LAGS : (2 * q + 1) * LAGS, :] = joined(
+                jnp.where(lane < LAGS, first, pltpu.roll(second, LAGS, 1))
+            )
+            flat[(2 * q + 1) * LAGS : (2 * q + 2) * LAGS, :] = joined(
+                jnp.where(lane < LAGS, pltpu.roll(first, LAGS, 1), second)
+            )
+        at = pl.ds(pl.multiple_of(step * GROUP, GROUP), GROUP)
+        for m in range(channels // 2):
+            out_ref[slot, at, m * 2 * LAGS : (m + 1) * 2 * LAGS] = flat[
+                pl.ds(m, GROUP, stride=channels // 2), :
+            ]
+        return carry
+
+    lax.fori_loop(0, slots * steps, finish, 0)
+
+    def sent(n, carry):
+        transfer(n, lax.rem(n, slots), lax.rem(me + 1, days), finals[0]).wait_send()
+        return carry
+
+    lax.fori_loop(0, (days - 1) * slots, sent, 0)
 
 
 def stacked(left, right, rows, days, width, used):
     slots, channels = left.shape[0], left.shape[1]
-    tall = channels // days * LAGS
+    share = channels // days
+    tall = share * LAGS
     copies = (days - 1) * slots
+    landings = max(days - 1, 4)
     cost = 2 * slots * channels * LAGS * left.shape[2] * channels
     return pl.pallas_call(
         functools.partial(stack_kernel, days, width, used),
-        out_shape=jax.ShapeDtypeStruct((slots, tall, channels), jnp.float32),
+        out_shape=jax.ShapeDtypeStruct((slots, share, channels * LAGS), jnp.float32),
         in_specs=[pl.BlockSpec(memory_space=pltpu.VMEM)] * 3,
         out_specs=pl.BlockSpec(memory_space=pltpu.VMEM),
         scratch_shapes=[
             pltpu.VMEM((copies, tall, channels), jnp.bfloat16),
-            pltpu.VMEM((copies, tall, channels), jnp.bfloat16),
+            pltpu.VMEM((landings, slots, tall, channels), jnp.bfloat16),
+            pltpu.VMEM((slots, tall, channels), jnp.float32),
+            pltpu.VMEM((tall, channels), jnp.float32),
+            pltpu.VMEM((GROUP // 2, channels, 2 * LAGS), jnp.float32),
+            pltpu.VMEM((GROUP * channels // 2, 2 * LAGS), jnp.float32),
             pltpu.SemaphoreType.DMA((copies,)),
-            pltpu.SemaphoreType.DMA((copies,)),
+            pltpu.SemaphoreType.DMA((landings, slots)),
         ],
         compiler_params=pltpu.CompilerParams(
             collective_id=0, has_side_effects=True, vmem_limit_bytes=48 * 1024 * 1024
@@ -198,15 +281,9 @@
     right = right.reshape(slots, channels, used, 2, width // CHUNK, CHUNK)
     right = right.transpose(0, 2, 4, 3, 5, 1).reshape(slots, used * 2 * width, channels)
 
-    summed = stacked(left, right, lag_rows(width, used), days, width, used)
-    summed = summed.reshape(slots, channels // days, LAGS, channels)
-    even, odd = summed[:, :, :HALF], summed[:, :, HALF:]
-    ahead = even[:, :, 1:] + odd[:, :, 1:]
-    behind = even[:, :, 1:] - odd[:, :, 1:]
-    lagged = jnp.concatenate([odd[:, :, :1], behind[:, :, ::-1], even[:, :, :1], ahead], 2)
-    alive = (jnp.arange(slots) < slot_count[0])[:, None, None, None]
-    lagged = jnp.where(alive, lagged, jnp.zeros_like(lagged))
-    return lagged.transpose(0, 1, 3, 2).reshape(slots, channels // days, channels * LAGS)
+    lagged = stacked(left, right, lag_rows(width, used), days, width, used)
+    alive = (jnp.arange(slots) < slot_count[0])[:, None, None]
+    return jnp.where(alive, lagged, jnp.zeros_like(lagged))
 
 
 def solution(mesh):

time: 229 us -> 138 us (0.60)
  local copies, waits for them, and re-layouts: 68 us -> 18.2 us
  Pallas kernels: 101 us -> 78.8 us
  other arithmetic: 29.9 us -> 12 us
    rev x1 -> x0, local copies, waits for them, and re-layouts: 34 us -> none  [per_device(): behind[:, :, ::-1]]
    pallas_call x1, Pallas kernels: 101 us -> 78.8 us  [stacked(): pl.pallas_call(functools.partial(stack_kernel, days, width, used), out_sh...]
    transpose x1 -> x0, other arithmetic: 11.1 us -> none  [per_device(): lagged.transpose(0, 1, 3, 2)]
    unnamed x9 -> x5, local copies, waits for them, and re-layouts: 13.3 us -> 2.75 us
    sub x1 -> x0, other arithmetic: 8.33 us -> none  [per_device(): behind = even[:, :, 1:] - odd[:, :, 1:]]
    reshape x1 -> x0, local copies, waits for them, and re-layouts: 4.76 us -> none  [per_device(): lagged.transpose(0, 1, 3, 2)]
  transfers between devices with their start and end apart: 3 -> 3, of which waited for: 2 -> 2; matrix products, arithmetic and copies ran while one was open for 0% -> 1% of each run, Pallas kernels for 0% -> 0%
where the time goes in v2:
time: 138 us; the launch traced here: 137 us
  Pallas kernels  78.8 us (57%)
  waiting for transfers between devices  22.9 us (17%)
  local copies, waits for them, and re-layouts  18.2 us (13%)
  other arithmetic  12 us (9%)
  starting transfers between devices  3.81 us (3%)
    pallas_call x1, Pallas kernels, stacked(): pl.pallas_call(functools.partial(stack_kernel, days, width, used), out_sh...  78.8 us
    ppermute x3, waiting for transfers between devices, swapped(): return lax.ppermute(value, 'pair', [(i, i ^ mask) for i in range(count)])  22.9 us
    gather x1, local copies, waits for them, and re-layouts, per_device(): left = jnp.take(pool, place[:, 0], axis=0).astype(jnp.float32)  4.19 us
    select_n x1, local copies, waits for them, and re-layouts, per_device(): right = jnp.take(pool, place[:, 1], axis=0)  4.08 us
    convert_element_type x1, other arithmetic, per_device(): left = jnp.take(pool, place[:, 0], axis=0).astype(jnp.float32)  3.9 us
    ppermute x3, starting transfers between devices, swapped(): return lax.ppermute(value, 'pair', [(i, i ^ mask) for i in range(count)])  3.81 us
    another operation x1, other arithmetic, gathered(): pool = jnp.stack([moved, swapped(moved, 1), far, swapped(far, 1)], 0)  3.4 us
    gather x1, local copies, waits for them, and re-layouts, per_device(): right = jnp.take(pool, place[:, 1], axis=0)  2.87 us
  transfers between devices with their start and end apart: 3, of which 2 were waited for; matrix products, arithmetic and copies ran while one was open for 1% of the time, Pallas kernels for 0%

profile of v2, /device:TPU:11, one launch (start us, length us, event | category | flops | bytes accessed | tf_op | source)
XLA Modules:
  0.0 136.5 jit_solution(10124335985191599963)
XLA Ops:
  0.0 0.7 fusion
  0.7 0.7 compare_and_fusion.2
  1.3 2.7 %copy.16 = bf16[1,128,4,2048]{3,1,2,0:T(8,128)(2,1)S(1)} copy(bf16[1,128,4,2048]{3,2,1,0:T(4,128)(2,1)} %param.7) | data formatting | bytes 4194304 | tf_op args[0]
  4.1 0.6 gather_fusion
  4.7 0.7 copy.9
  5.4 0.5 copy.12
  6.0 0.1 broadcast_select_fusion.2
  6.1 1.3 collective-permute-start.1
  7.5 1.0 collective-permute-start
  8.4 0.5 copy.10
  9.6 0.2 slice_reduce_fusion
  9.8 20.5 %collective-permute-done.1 = bf16[128,4096]{1,0:T(8,128)(2,1)} collective-permute-done((bf16[128,4096]{1,0:T(8,128)(2,1)S(1)}, bf16[128,4096]{1,0:T(8,128)(2,1)}, u32[]{:S(2)}, u32[]{:S(2)}) %collective-permute-start.1) | collective-permute-done | bytes 1048608 | tf_op jit(solution)/shard_map/ppermute | solution.py:255
  30.3 1.5 %collective-permute-start.2 = (bf16[128,4096]{1,0:T(8,128)(2,1)}, bf16[128,4096]{1,0:T(8,128)(2,1)S(1)}, u32[]{:S(2)}, u32[]{:S(2)}) collective-permute-start(bf16[128,4096]{1,0:T(8,128)(2,1)} %collective-permute-done.1), channel_id=1, source_target_pairs={{0,4},{4,0},{8,12},{12,8},{1,5},{5,1},{9,13},{13,9},{2,6},{6,2},{1... | collective-permute-start | bytes 3145736 | tf_op jit(solution)/shard_map/ppermute | solution.py:255
  31.9 0.1 broadcast_select_fusion.3
  32.0 2.4 %collective-permute-done.2 = bf16[128,4096]{1,0:T(8,128)(2,1)S(1)} collective-permute-done((bf16[128,4096]{1,0:T(8,128)(2,1)}, bf16[128,4096]{1,0:T(8,128)(2,1)S(1)}, u32[]{:S(2)}, u32[]{:S(2)}) %collective-permute-start.2) | collective-permute-done | bytes 1048608 | tf_op jit(solution)/shard_map/ppermute | solution.py:255
  34.4 3.4 %pad_maximum_fusion = bf16[4,128,4096]{2,1,0:T(8,128)(2,1)} fusion(bf16[1,128,4096]{2,1,0:T(8,128)(2,1)S(1)} %bitcast.29, bf16[1,128,4096]{2,1,0:T(8,128)(2,1)} %bitcast.10, bf16[1,128,4096]{2,1,0:T(8,128)(2,1)} %bitcast.9, bf16[1,128,4096]{2,1,0:T(8,128)(2,1)S(1)} %broadcast_select_fusion.3), kind=kLoop, calls=%fused_computation.3 | loop fusion | flops 6291456 | bytes 8388608 | tf_op jit(solution)/shard_map/stack | solution.py:262
  37.8 2.9 %gather_fusion.2 = bf16[2,128,4096]{2,1,0:T(8,128)(2,1)S(1)} fusion(bf16[4,128,4096]{2,1,0:T(8,128)(2,1)} %pad_maximum_fusion, s32[1024]{0:T(1024)S(1)} %pad_clamp_fusion), kind=kCustom, calls=%fused_computation.1.clone | custom fusion | bytes 4194312 | tf_op jit(solution)/shard_map/jit(_take)/gather | solution.py:280
  40.7 1.6 %broadcast_select_fusion = bf16[2,128,4096]{2,1,0:T(8,128)(2,1)} fusion(bf16[2,128,4096]{2,1,0:T(8,128)(2,1)S(1)} %gather_fusion.2, pred[2]{0:T(512)(128)(4,1)S(1)} %get-tuple-element.10), kind=kLoop, calls=%fused_computation.6 | loop fusion | flops 1048576 | bytes 4194306 | tf_op jit(solution)/shard_map/jit(_take)/select_n | solution.py:280
  42.3 4.1 %copy.13 = bf16[2,128,4096]{1,2,0:T(8,128)(2,1)} copy(bf16[2,128,4096]{2,1,0:T(8,128)(2,1)} %broadcast_select_fusion) | data formatting | bytes 4194304 | tf_op jit(solution)/shard_map/jit(_take)/select_n | solution.py:280
  46.3 1.7 %copy.14 = bf16[2,2,4,2,256,128]{5,4,3,2,1,0:T(8,128)(2,1)S(1)} copy(bf16[2,2,4,2,256,128]{5,4,2,3,1,0:T(8,128)(2,1)} %bitcast.26) | data formatting | bytes 4194304 | tf_op jit(solution)/shard_map/transpose | solution.py:282
  48.1 4.2 %gather_fusion.1 = bf16[2,128,4096]{2,1,0:T(8,128)(2,1)} fusion(bf16[4,128,4096]{2,1,0:T(8,128)(2,1)} %pad_maximum_fusion, s32[1024]{0:T(1024)S(1)} %pad_clamp_fusion.1), kind=kCustom, calls=%fused_computation.clone | custom fusion | bytes 4194312 | tf_op jit(solution)/shard_map/jit(_take)/gather | solution.py:279
  52.3 3.9 %select_convert_fusion.left_ref = f32[2,128,4096]{2,1,0:T(8,128)} fusion(bf16[2,128,4096]{2,1,0:T(8,128)(2,1)} %gather_fusion.1, pred[2]{0:T(512)(128)(4,1)S(1)} %get-tuple-element.11), kind=kLoop, calls=%fused_computation.5 | loop fusion | flops 2097152 | bytes 6291458 | tf_op jit(solution)/shard_map/convert_element_type | solution.py:279
  56.2 78.8 %shard_map.55 = f32[2,32,8192]{2,1,0:T(8,128)S(1)} custom-call(f32[2,128,4096]{2,1,0:T(8,128)} %select_convert_fusion.left_ref, bf16[2,4096,128]{2,1,0:T(8,128)(2,1)S(1)} %bitcast.23, bf16[80,1024]{1,0:T(8,128)(2,1)S(1)} %copy-done), custom_call_target="tpu_custom_call" | custom-call | flops 17179869184 | bytes 8388608 | tf_op jit(solution)/shard_map/pallas_call | solution.py:225
  135.0 1.5 %broadcast_select_fusion.1 = f32[2,32,8192]{2,1,0:T(8,128)} fusion(f32[2,32,8192]{2,1,0:T(8,128)S(1)} %shard_map.55, pred[2]{0:T(512)(128)(4,1)S(1)} %iota_compare_fusion), kind=kLoop, calls=%fused_computation.7 | loop fusion | flops 524288 | bytes 4194306 | tf_op jit(solution)/shard_map/jit(_where)/select_n | solution.py:286
  (14 shorter events, 0.2 us)
Async XLA Ops:
  6.0 3.6 %copy-start.1 = (s32[1,2,2]{2,1,0:T(2,128)S(1)}, s32[1,2,2]{2,1,0:T(2,128)}, u32[]{:S(2)}) copy-start(s32[1,2,2]{2,1,0:T(2,128)} %param.9) | copy-start | bytes 52
  6.1 24.2 %collective-permute-start.1 = (bf16[128,4096]{1,0:T(8,128)(2,1)S(1)}, bf16[128,4096]{1,0:T(8,128)(2,1)}, u32[]{:S(2)}, u32[]{:S(2)}) collective-permute-start(bf16[128,4096]{1,0:T(8,128)(2,1)S(1)} %broadcast_select_fusion.2), channel_id=1, source_target_pairs={{0,8},{4,12},{8,0},{12,4},{1,9},{5,13},{9,1},{13,5},{2,10},{6,14},... | collective-permute-start | bytes 3145736 | tf_op jit(solution)/shard_map/ppermute | solution.py:255
  7.5 24.6 %collective-permute-start = (bf16[128,4096]{1,0:T(8,128)(2,1)S(1)}, bf16[128,4096]{1,0:T(8,128)(2,1)}, u32[]{:S(2)}, u32[]{:S(2)}) collective-permute-start(bf16[128,4096]{1,0:T(8,128)(2,1)S(1)} %broadcast_select_fusion.2), channel_id=1, source_target_pairs={{0,4},{4,0},{8,12},{12,8},{1,5},{5,1},{9,13},{13,9},{2,6},{6,2},{1... | collective-permute-start | bytes 3145736 | tf_op jit(solution)/shard_map/ppermute | solution.py:255
  30.3 4.0 %collective-permute-start.2 = (bf16[128,4096]{1,0:T(8,128)(2,1)}, bf16[128,4096]{1,0:T(8,128)(2,1)S(1)}, u32[]{:S(2)}, u32[]{:S(2)}) collective-permute-start(bf16[128,4096]{1,0:T(8,128)(2,1)} %collective-permute-done.1), channel_id=1, source_target_pairs={{0,4},{4,0},{8,12},{12,8},{1,5},{5,1},{9,13},{13,9},{2,6},{6,2},{1... | collective-permute-start | bytes 3145736 | tf_op jit(solution)/shard_map/ppermute | solution.py:255
  52.3 3.9 %copy-start = (bf16[80,1024]{1,0:T(8,128)(2,1)S(1)}, bf16[80,1024]{1,0:T(8,128)(2,1)}, u32[]{:S(2)}) copy-start(bf16[80,1024]{1,0:T(8,128)(2,1)} %constant.35.clone.rows_ref) | copy-start | bytes 491524

commit v3 on v2

--- a/solution.py
+++ b/solution.py
@@ -90,9 +90,41 @@
     return piece
 
 
+def fill_pool(near_ref, pool, ready, near_send, near_recv):
+    here = lax.axis_index("pair")
+    sibling, across = here + 1 - 2 * lax.rem(here, 2), lax.rem(here + 2, 4)
+    tall = near_ref.shape[1] // 2
+
+    def move(n, source, place, part, target):
+        at = pl.ds(part * tall, tall)
+        return pltpu.make_async_remote_copy(
+            src_ref=source.at[at],
+            dst_ref=pool.at[place, at],
+            send_sem=near_send.at[n],
+            recv_sem=near_recv.at[n],
+            device_id={"pair": target},
+            device_id_type=MESH,
+        )
+
+    far = [move(h, near_ref.at[0], 2, h, across) for h in range(2)]
+    beside = [move(2 + h, near_ref.at[0], 1, h, sibling) for h in range(2)]
+    passed = [move(4 + h, pool.at[2], 3, h, sibling) for h in range(2)]
+    ready()
+    for copy in far + beside:
+        copy.start()
+    pool[0] = near_ref[0]
+    for h in range(2):
+        far[h].wait_recv()
+        passed[h].start()
+    for copy in beside + passed:
+        copy.wait_recv()
+    return far + beside + passed
+
+
 def stack_kernel(
-    days, width, used, left_ref, right_ref, rows_ref, out_ref,
-    send, recv, own, fresh, turned, flat, send_sem, recv_sem,
+    days, owners, width, used, near_ref, place_ref, rows_ref, out_ref,
+    send, recv, own, fresh, turned, flat, left_ref, right_ref, pool, send_sem, recv_sem,
+    near_send, near_recv,
 ):
     slots, channels = left_ref.shape[0], left_ref.shape[1]
     share = channels // days
@@ -107,6 +139,33 @@
         pl.semaphore_signal(
             barrier, inc=1, device_id={"day": lax.rem(me + by, days)}, device_id_type=MESH
         )
+    moves = []
+    if owners == 4:
+        here = lax.axis_index("pair")
+        for peer in (here + 1 - 2 * lax.rem(here, 2), lax.rem(here + 2, 4)):
+            pl.semaphore_signal(barrier, inc=1, device_id={"pair": peer}, device_id_type=MESH)
+        moves = fill_pool(
+            near_ref, pool, lambda: pl.semaphore_wait(barrier, days + 1), near_send, near_recv
+        )
+        blocks = pool
+    else:
+        pl.semaphore_wait(barrier, days - 1)
+        blocks = near_ref
+
+    def unpack(slot, carry):
+        a, b = place_ref[slot, 0], place_ref[slot, 1]
+        for r in range(0, channels, 16):
+            left_ref[slot, r : r + 16, :] = blocks[a, r : r + 16, :].astype(jnp.float32)
+        parts = CHUNK // 128
+        for sub in range(used):
+            for e in range(2):
+                for f in range(width // 128):
+                    source = (sub * 2 + e) * width + f * 128
+                    to = ((sub * (width // CHUNK) + f // parts) * 2 + e) * CHUNK + f % parts * 128
+                    right_ref[slot, to : to + 128, :] = blocks[b, :, source : source + 128].T
+        return carry
+
+    lax.fori_loop(0, slots, unpack, 0)
 
     def transfer(n, slot, target, landing):
         return pltpu.make_async_remote_copy(
@@ -147,10 +206,6 @@
                 send[n] = fresh[...].astype(jnp.bfloat16)
         else:
             send[n] = fresh[...].astype(jnp.bfloat16)
-
-        @pl.when(n == 0)
-        def _():
-            pl.semaphore_wait(barrier, days - 1)
 
         transfer(n, slot, target, landing).start()
         return carry
@@ -213,19 +268,25 @@
         return carry
 
     lax.fori_loop(0, (days - 1) * slots, sent, 0)
-
-
-def stacked(left, right, rows, days, width, used):
-    slots, channels = left.shape[0], left.shape[1]
+    for copy in moves:
+        copy.wait_send()
+
+
+def stacked(near, place, rows, days, owners, width, used):
+    slots, channels, depth = place.shape[0], near.shape[1], near.shape[2]
     share = channels // days
     tall = share * LAGS
     copies = (days - 1) * slots
     landings = max(days - 1, 4)
-    cost = 2 * slots * channels * LAGS * left.shape[2] * channels
+    cost = 2 * slots * channels * LAGS * depth * channels
     return pl.pallas_call(
-        functools.partial(stack_kernel, days, width, used),
+        functools.partial(stack_kernel, days, owners, width, used),
         out_shape=jax.ShapeDtypeStruct((slots, share, channels * LAGS), jnp.float32),
-        in_specs=[pl.BlockSpec(memory_space=pltpu.VMEM)] * 3,
+        in_specs=[
+            pl.BlockSpec(memory_space=pltpu.VMEM),
+            pl.BlockSpec(memory_space=pltpu.SMEM),
+            pl.BlockSpec(memory_space=pltpu.VMEM),
+        ],
         out_specs=pl.BlockSpec(memory_space=pltpu.VMEM),
         scratch_shapes=[
             pltpu.VMEM((copies, tall, channels), jnp.bfloat16),
@@ -234,14 +295,19 @@
             pltpu.VMEM((tall, channels), jnp.float32),
             pltpu.VMEM((GROUP // 2, channels, 2 * LAGS), jnp.float32),
             pltpu.VMEM((GROUP * channels // 2, 2 * LAGS), jnp.float32),
+            pltpu.VMEM((slots, channels, depth), jnp.float32),
+            pltpu.VMEM((slots, depth, channels), jnp.bfloat16),
+            pltpu.VMEM((4 if owners == 4 else 1, channels, depth), jnp.bfloat16),
             pltpu.SemaphoreType.DMA((copies,)),
             pltpu.SemaphoreType.DMA((landings, slots)),
+            pltpu.SemaphoreType.DMA((6,)),
+            pltpu.SemaphoreType.DMA((6,)),
         ],
         compiler_params=pltpu.CompilerParams(
             collective_id=0, has_side_effects=True, vmem_limit_bytes=48 * 1024 * 1024
         ),
         cost_estimate=pl.CostEstimate(flops=cost, bytes_accessed=1 << 23, transcendentals=0),
-    )(left, right, rows)
+    )(near, place, rows)
 
 
 def passed_along(value, by):
@@ -250,17 +316,10 @@
     return lax.ppermute(value, "pair", pairs)
 
 
-def swapped(value, mask):
-    count = lax.axis_size("pair")
-    return lax.ppermute(value, "pair", [(i, i ^ mask) for i in range(count)])
-
-
 def gathered(moved, wanted):
     here = lax.axis_index("pair")
     if lax.axis_size("pair") == 4:
-        far = swapped(moved, 2)
-        pool = jnp.stack([moved, swapped(moved, 1), far, swapped(far, 1)], 0)
-        return pool, wanted ^ here
+        return moved[None], wanted ^ here
     nearby = [
         moved if step == 0 else passed_along(moved, -step) for step in range(-REACH, REACH + 1)
     ]
@@ -275,13 +334,9 @@
     moved = jnp.take(local, picks, axis=1).reshape(channels, used * 2 * width)
     pairs = pair_list[0]
     slots = pairs.shape[0]
-    pool, place = gathered(moved, pairs)
-    left = jnp.take(pool, place[:, 0], axis=0).astype(jnp.float32)
-    right = jnp.take(pool, place[:, 1], axis=0)
-    right = right.reshape(slots, channels, used, 2, width // CHUNK, CHUNK)
-    right = right.transpose(0, 2, 4, 3, 5, 1).reshape(slots, used * 2 * width, channels)
-
-    lagged = stacked(left, right, lag_rows(width, used), days, width, used)
+    near, place = gathered(moved, pairs)
+    owners = lax.axis_size("pair")
+    lagged = stacked(near, place, lag_rows(width, used), days, owners, width, used)
     alive = (jnp.arange(slots) < slot_count[0])[:, None, None]
     return jnp.where(alive, lagged, jnp.zeros_like(lagged))
 

time: 138 us -> 116 us (0.84)
  Pallas kernels: 78.8 us -> 108 us
  waiting for transfers between devices: 22.9 us -> 0 us
  local copies, waits for them, and re-layouts: 18.2 us -> 5.4 us
  other arithmetic: 12 us -> 1.69 us
  starting transfers between devices: 3.81 us -> 0 us
    pallas_call x1, Pallas kernels: 78.8 us -> 108 us  [stacked(): pl.pallas_call(functools.partial(stack_kernel, days, owners, width, used)...]
    ppermute x3 -> x0, waiting for transfers between devices: 22.9 us -> none  [swapped(): return lax.ppermute(value, 'pair', [(i, i ^ mask) for i in range(count)])]
    gather x2 -> x0, local copies, waits for them, and re-layouts: 7.05 us -> none  [the longest x1 4.19 us: per_device(): left = jnp.take(pool, place[:, 0], axis=0).astype(jnp.float32)]
    select_n x1 -> x0, local copies, waits for them, and re-layouts: 4.08 us -> none  [per_device(): right = jnp.take(pool, place[:, 1], axis=0)]
    convert_element_type x1 -> x0, other arithmetic: 3.9 us -> none  [per_device(): left = jnp.take(pool, place[:, 0], axis=0).astype(jnp.float32)]
    ppermute x3 -> x0, starting transfers between devices: 3.81 us -> none  [swapped(): return lax.ppermute(value, 'pair', [(i, i ^ mask) for i in range(count)])]
    another operation x1 -> x0, other arithmetic: 3.4 us -> none  [gathered(): pool = jnp.stack([moved, swapped(moved, 1), far, swapped(far, 1)], 0)]
    transpose x1 -> x0, local copies, waits for them, and re-layouts: 1.73 us -> none  [per_device(): right.transpose(0, 2, 4, 3, 5, 1).reshape(slots, used * 2 * width, channels)]
  transfers between devices with their start and end apart: 3 -> 0, of which waited for: 2 -> 0; matrix products, arithmetic and copies ran while one was open for 1% -> 0% of each run, Pallas kernels for 0% -> 0%
where the time goes in v3:
time: 116 us
  Pallas kernels  108 us (93%)
  local copies, waits for them, and re-layouts  5.4 us (5%)
  other arithmetic  1.69 us (1%)
    pallas_call x1, Pallas kernels, stacked(): pl.pallas_call(functools.partial(stack_kernel, days, owners, width, used)...  108 us
    unnamed x7, local copies, waits for them, and re-layouts  2.77 us
    gather x3, local copies, waits for them, and re-layouts, per_device(): moved = jnp.take(local, picks, axis=1).reshape(channels, used * 2 * width)  2.52 us

profile of v3, /device:TPU:11, one launch (start us, length us, event | category | flops | bytes accessed | tf_op | source)
XLA Modules:
  0.0 115.5 jit_solution(2193362328177228866)
XLA Ops:
  0.0 0.0 copy-start.2
  0.0 2.8 %copy.9 = bf16[1,128,4,2048]{3,1,2,0:T(8,128)(2,1)S(1)} copy(bf16[1,128,4,2048]{3,2,1,0:T(4,128)(2,1)} %param.5) | data formatting | bytes 4194304 | tf_op args[0]
  2.8 0.0 copy-done.2
  2.8 0.6 gather_fusion
  3.4 1.1 copy.7
  4.5 0.0 copy-start.1
  4.5 0.0 copy-start
  4.5 0.8 gather.7
  5.4 0.1 broadcast_in_dim.27
  5.5 0.1 broadcast_select_fusion.1.near_ref
  5.6 0.0 copy-done.1
  5.6 0.0 copy-done
  5.6 107.7 %shard_map.55 = f32[2,32,8192]{2,1,0:T(8,128)S(1)} custom-call(bf16[1,128,4096]{2,1,0:T(8,128)(2,1)S(1)} %broadcast_select_fusion.1.near_ref, s32[2,2]{1,0:T(2,128)S(1)} %xor_bitcast_fusion.place_ref, bf16[80,1024]{1,0:T(8,128)(2,1)S(1)} %copy-done), custom_call_target="tpu_custom_call" | custom-call | flops 17179869184 | bytes 8388608 | tf_op jit(solution)/shard_map/pallas_call | solution.py:282
  114.0 1.5 %broadcast_select_fusion = f32[2,32,8192]{2,1,0:T(8,128)} fusion(f32[2,32,8192]{2,1,0:T(8,128)S(1)} %shard_map.55, pred[2]{0:T(512)(128)(4,1)S(1)} %iota_compare_fusion), kind=kLoop, calls=%fused_computation.2 | loop fusion | flops 524288 | bytes 4194306 | tf_op jit(solution)/shard_map/jit(_where)/select_n | solution.py:341
  (6 shorter events, 0.1 us)
Async XLA Ops:
  0.0 2.8 %copy-start.2 = (s32[1,2]{1,0:T(1,128)S(1)}, s32[1,2]{1,0:T(1,128)}, u32[]{:S(2)}) copy-start(s32[1,2]{1,0:T(1,128)} %param.6) | copy-start | bytes 28
  4.5 1.1 copy-start.1
  4.5 1.1 copy-start

commit v4 on v3

--- a/solution.py
+++ b/solution.py
@@ -11,7 +11,7 @@
 LAGS = 64
 HALF = LAGS // 2
 REACH = 3
-GROUP = 8
+GROUP = 16
 CHUNK = 256
 MESH = pl.DeviceIdType.MESH
 
@@ -121,11 +121,34 @@
     return far + beside + passed
 
 
+def helper_moves(near_ref, lent, me, lent_send, lent_recv):
+    here = lax.axis_index("pair")
+    sibling, across = here + 1 - 2 * lax.rem(here, 2), lax.rem(here + 2, 4)
+
+    def move(n, source, place, device):
+        return pltpu.make_async_remote_copy(
+            src_ref=source,
+            dst_ref=lent.at[place],
+            send_sem=lent_send.at[n],
+            recv_sem=lent_recv.at[n],
+            device_id=device,
+            device_id_type=MESH,
+        )
+
+    return [
+        move(0, near_ref.at[0], 0, {"day": 1 + me // 2}),
+        move(1, lent.at[0], 2, {"pair": across}),
+        move(2, lent.at[0], 1, {"pair": sibling}),
+        move(3, lent.at[2], 3, {"pair": sibling}),
+    ]
+
+
 def stack_kernel(
     days, owners, width, used, near_ref, place_ref, rows_ref, out_ref,
     send, recv, own, fresh, turned, flat, left_ref, right_ref, pool, send_sem, recv_sem,
-    near_send, near_recv,
+    near_send, near_recv, lent, lent_send, lent_recv,
 ):
+    helped = days == 4 and owners == 4
     slots, channels = left_ref.shape[0], left_ref.shape[1]
     share = channels // days
     steps = share // GROUP
@@ -140,19 +163,37 @@
             barrier, inc=1, device_id={"day": lax.rem(me + by, days)}, device_id_type=MESH
         )
     moves = []
+    inner = lax.rem((me + 1) // 2, 2) == 1
+    if helped:
+        lend, lent_across, lent_beside, lent_passed = helper_moves(
+            near_ref, lent, me, lent_send, lent_recv
+        )
+
+    def ready():
+        pl.semaphore_wait(barrier, days + 1)
+        if helped:
+            @pl.when(jnp.logical_not(inner))
+            def _():
+                lend.start()
+
     if owners == 4:
         here = lax.axis_index("pair")
         for peer in (here + 1 - 2 * lax.rem(here, 2), lax.rem(here + 2, 4)):
             pl.semaphore_signal(barrier, inc=1, device_id={"pair": peer}, device_id_type=MESH)
-        moves = fill_pool(
-            near_ref, pool, lambda: pl.semaphore_wait(barrier, days + 1), near_send, near_recv
-        )
+        moves = fill_pool(near_ref, pool, ready, near_send, near_recv)
         blocks = pool
     else:
         pl.semaphore_wait(barrier, days - 1)
         blocks = near_ref
 
-    def unpack(slot, carry):
+    if helped:
+        @pl.when(inner)
+        def _():
+            lend.wait_recv()
+            lent_across.start()
+            lent_beside.start()
+
+    def unpack(blocks, slot):
         a, b = place_ref[slot, 0], place_ref[slot, 1]
         for r in range(0, channels, 16):
             left_ref[slot, r : r + 16, :] = blocks[a, r : r + 16, :].astype(jnp.float32)
@@ -163,9 +204,12 @@
                     source = (sub * 2 + e) * width + f * 128
                     to = ((sub * (width // CHUNK) + f // parts) * 2 + e) * CHUNK + f % parts * 128
                     right_ref[slot, to : to + 128, :] = blocks[b, :, source : source + 128].T
+
+    def unpack_own(slot, carry):
+        unpack(blocks, slot)
         return carry
 
-    lax.fori_loop(0, slots, unpack, 0)
+    lax.fori_loop(0, slots, unpack_own, 0)
 
     def transfer(n, slot, target, landing):
         return pltpu.make_async_remote_copy(
@@ -185,13 +229,13 @@
             left_ref, right_ref, rows_ref, slot, owner * share + step * GROUP, width, used
         )
 
-    def send_piece(n, carry):
+    def send_piece(n):
         k, slot = n // slots, lax.rem(n, slots)
         owner, target, landing, adds = piece(k)
 
-        def one(step, inner):
+        def one(step, carry):
             fresh[span(step), :] = block(slot, owner, step)
-            return inner
+            return carry
 
         lax.fori_loop(0, steps, one, 0)
 
@@ -208,16 +252,44 @@
             send[n] = fresh[...].astype(jnp.bfloat16)
 
         transfer(n, slot, target, landing).start()
-        return carry
-
-    lax.fori_loop(0, (days - 1) * slots, send_piece, 0)
 
     def own_piece(n, carry):
         slot, step = n // steps, lax.rem(n, steps)
         own[slot, span(step), :] = block(slot, me, step)
         return carry
 
-    lax.fori_loop(0, slots * steps, own_piece, 0)
+    def send_one(n, carry):
+        send_piece(n)
+        return carry
+
+    copies = (days - 1) * slots
+    last = slots - 1
+    if helped:
+        lax.fori_loop(0, copies - slots, send_one, 0)
+
+        @pl.when(inner)
+        def _():
+            lent_across.wait_recv()
+            lent_passed.start()
+
+        lax.fori_loop(0, slots * steps, own_piece, 0)
+        lax.fori_loop(copies - slots, copies - 1, send_one, 0)
+
+        @pl.when(inner)
+        def _():
+            send_piece(copies - 1)
+            lent_beside.wait_recv()
+            lent_passed.wait_recv()
+            unpack(lent, last)
+
+            def extra(step, carry):
+                recv[2, last, span(step), :] = block(last, me, step).astype(jnp.bfloat16)
+                return carry
+
+            lax.fori_loop(0, steps, extra, 0)
+    else:
+        lax.fori_loop(0, copies, send_one, 0)
+        lax.fori_loop(0, slots * steps, own_piece, 0)
 
     lane = lax.broadcasted_iota(jnp.int32, (LAGS, 2 * LAGS), 1)
     lag = lane % LAGS
@@ -235,9 +307,15 @@
     def finish(n, carry):
         slot, step = n // steps, lax.rem(n, steps)
 
-        @pl.when(step == 0)
-        def _():
-            for f in finals:
+        for f in finals:
+            landed = step == 0
+            if helped and f == 2:
+                landed = jnp.logical_and(
+                    landed, jnp.logical_not(jnp.logical_and(inner, slot == last))
+                )
+
+            @pl.when(landed)
+            def _():
                 transfer(0, slot, lax.rem(me + 1, days), f).wait_recv()
 
         total = own[slot, span(step), :]
@@ -267,7 +345,21 @@
         transfer(n, lax.rem(n, slots), lax.rem(me + 1, days), finals[0]).wait_send()
         return carry
 
-    lax.fori_loop(0, (days - 1) * slots, sent, 0)
+    if helped:
+        lax.fori_loop(0, copies - 1, sent, 0)
+
+        @pl.when(inner)
+        def _():
+            sent(copies - 1, 0)
+            lent_across.wait_send()
+            lent_beside.wait_send()
+            lent_passed.wait_send()
+
+        @pl.when(jnp.logical_not(inner))
+        def _():
+            lend.wait_send()
+    else:
+        lax.fori_loop(0, copies, sent, 0)
     for copy in moves:
         copy.wait_send()
 
@@ -302,6 +394,9 @@
             pltpu.SemaphoreType.DMA((landings, slots)),
             pltpu.SemaphoreType.DMA((6,)),
             pltpu.SemaphoreType.DMA((6,)),
+            pltpu.VMEM((4 if owners == 4 else 1, channels, depth), jnp.bfloat16),
+            pltpu.SemaphoreType.DMA((4,)),
+            pltpu.SemaphoreType.DMA((4,)),
         ],
         compiler_params=pltpu.CompilerParams(
             collective_id=0, has_side_effects=True, vmem_limit_bytes=48 * 1024 * 1024

time: 116 us -> 110 us (0.948)
  Pallas kernels: 108 us -> 102 us
    pallas_call x1, Pallas kernels: 108 us -> 102 us  [stacked(): pl.pallas_call(functools.partial(stack_kernel, days, owners, width, used)...]
where the time goes in v4:
time: 110 us
  Pallas kernels  102 us (93%)
  local copies, waits for them, and re-layouts  5.4 us (5%)
  other arithmetic  1.69 us (2%)
    pallas_call x1, Pallas kernels, stacked(): pl.pallas_call(functools.partial(stack_kernel, days, owners, width, used)...  102 us
    unnamed x7, local copies, waits for them, and re-layouts  2.77 us
    gather x3, local copies, waits for them, and re-layouts, per_device(): moved = jnp.take(local, picks, axis=1).reshape(channels, used * 2 * width)  2.52 us

profile of v4, /device:TPU:11, one launch (start us, length us, event | category | flops | bytes accessed | tf_op | source)
XLA Modules:
  0.0 109.6 jit_solution(4910841985589222875)
XLA Ops:
  0.0 0.0 copy-start.2
  0.0 2.8 %copy.9 = bf16[1,128,4,2048]{3,1,2,0:T(8,128)(2,1)S(1)} copy(bf16[1,128,4,2048]{3,2,1,0:T(4,128)(2,1)} %param.5) | data formatting | bytes 4194304 | tf_op args[0]
  2.8 0.0 copy-done.2
  2.8 0.6 gather_fusion
  3.4 1.1 copy.7
  4.5 0.0 copy-start.1
  4.5 0.0 copy-start
  4.5 0.8 gather.7
  5.4 0.1 broadcast_in_dim.27
  5.5 0.1 broadcast_select_fusion.1.near_ref
  5.6 0.0 copy-done.1
  5.6 0.0 copy-done
  5.6 101.7 %shard_map.55 = f32[2,32,8192]{2,1,0:T(8,128)S(1)} custom-call(bf16[1,128,4096]{2,1,0:T(8,128)(2,1)S(1)} %broadcast_select_fusion.1.near_ref, s32[2,2]{1,0:T(2,128)S(1)} %xor_bitcast_fusion.place_ref, bf16[80,1024]{1,0:T(8,128)(2,1)S(1)} %copy-done), custom_call_target="tpu_custom_call" | custom-call | flops 17179869184 | bytes 8388608 | tf_op jit(solution)/shard_map/pallas_call | solution.py:374
  108.0 1.5 %broadcast_select_fusion = f32[2,32,8192]{2,1,0:T(8,128)} fusion(f32[2,32,8192]{2,1,0:T(8,128)S(1)} %shard_map.55, pred[2]{0:T(512)(128)(4,1)S(1)} %iota_compare_fusion), kind=kLoop, calls=%fused_computation.2 | loop fusion | flops 524288 | bytes 4194306 | tf_op jit(solution)/shard_map/jit(_where)/select_n | solution.py:436
  (6 shorter events, 0.1 us)
Async XLA Ops:
  0.0 2.8 %copy-start.2 = (s32[1,2]{1,0:T(1,128)S(1)}, s32[1,2]{1,0:T(1,128)}, u32[]{:S(2)}) copy-start(s32[1,2]{1,0:T(1,128)} %param.6) | copy-start | bytes 28
  4.5 1.1 %copy-start.1 = (s32[1,2,2]{2,1,0:T(2,128)S(1)}, s32[1,2,2]{2,1,0:T(2,128)}, u32[]{:S(2)}) copy-start(s32[1,2,2]{2,1,0:T(2,128)} %param.7) | copy-start | bytes 52
  4.5 1.1 %copy-start = (bf16[80,1024]{1,0:T(8,128)(2,1)S(1)}, bf16[80,1024]{1,0:T(8,128)(2,1)}, u32[]{:S(2)}) copy-start(bf16[80,1024]{1,0:T(8,128)(2,1)} %constant.25.clone.rows_ref) | copy-start | bytes 491524

commit v5 on v4

--- a/solution.py
+++ b/solution.py
@@ -229,9 +229,33 @@
             left_ref, right_ref, rows_ref, slot, owner * share + step * GROUP, width, used
         )
 
-    def send_piece(n):
-        k, slot = n // slots, lax.rem(n, slots)
+    copies = (days - 1) * slots
+    last = slots - 1
+    before = copies - slots if helped else copies
+    jobs = before + slots + (slots + 1 if helped else 0)
+
+    def job(n):
+        is_own = jnp.logical_and(n >= before, n < before + slots)
+        is_extra = n >= copies + slots
+        at_home = jnp.logical_or(is_own, is_extra)
+        sends = jnp.logical_not(at_home)
+        out = jnp.where(n < before, n, jnp.minimum(jnp.maximum(n - slots, 0), copies - 1))
+        k = out // slots
+        slot = jnp.where(is_extra, last, lax.rem(n, slots))
         owner, target, landing, adds = piece(k)
+        owner = jnp.where(at_home, me, owner)
+
+        if helped:
+            @pl.when(jnp.logical_and(inner, n == before))
+            def _():
+                lent_across.wait_recv()
+                lent_passed.start()
+
+            @pl.when(is_extra)
+            def _():
+                lent_beside.wait_recv()
+                lent_passed.wait_recv()
+                unpack(lent, last)
 
         def one(step, carry):
             fresh[span(step), :] = block(slot, owner, step)
@@ -239,70 +263,57 @@
 
         lax.fori_loop(0, steps, one, 0)
 
+        @pl.when(is_own)
+        def _():
+            own[slot] = fresh[...]
+
+        if helped:
+            @pl.when(is_extra)
+            def _():
+                recv[2, last] = fresh[...].astype(jnp.bfloat16)
+
         if days == 4:
-            @pl.when(adds)
-            def _():
-                transfer(n, slot, target, k - 1).wait_recv()
-                send[n] = (fresh[...] + recv[k - 1, slot].astype(jnp.float32)).astype(jnp.bfloat16)
-
-            @pl.when(jnp.logical_not(adds))
-            def _():
-                send[n] = fresh[...].astype(jnp.bfloat16)
+            @pl.when(jnp.logical_and(sends, adds))
+            def _():
+                transfer(out, slot, target, k - 1).wait_recv()
+                send[out] = (fresh[...] + recv[k - 1, slot].astype(jnp.float32)).astype(
+                    jnp.bfloat16
+                )
+
+            @pl.when(jnp.logical_and(sends, jnp.logical_not(adds)))
+            def _():
+                send[out] = fresh[...].astype(jnp.bfloat16)
         else:
-            send[n] = fresh[...].astype(jnp.bfloat16)
-
-        transfer(n, slot, target, landing).start()
-
-    def own_piece(n, carry):
-        slot, step = n // steps, lax.rem(n, steps)
-        own[slot, span(step), :] = block(slot, me, step)
+            @pl.when(sends)
+            def _():
+                send[out] = fresh[...].astype(jnp.bfloat16)
+
+        @pl.when(sends)
+        def _():
+            transfer(out, slot, target, landing).start()
+
+    def run(n, carry):
+        if helped:
+            pl.when(jnp.logical_or(inner, n < jobs - 2))(lambda: job(n))
+        else:
+            job(n)
         return carry
 
-    def send_one(n, carry):
-        send_piece(n)
-        return carry
-
-    copies = (days - 1) * slots
-    last = slots - 1
-    if helped:
-        lax.fori_loop(0, copies - slots, send_one, 0)
-
-        @pl.when(inner)
-        def _():
-            lent_across.wait_recv()
-            lent_passed.start()
-
-        lax.fori_loop(0, slots * steps, own_piece, 0)
-        lax.fori_loop(copies - slots, copies - 1, send_one, 0)
-
-        @pl.when(inner)
-        def _():
-            send_piece(copies - 1)
-            lent_beside.wait_recv()
-            lent_passed.wait_recv()
-            unpack(lent, last)
-
-            def extra(step, carry):
-                recv[2, last, span(step), :] = block(last, me, step).astype(jnp.bfloat16)
-                return carry
-
-            lax.fori_loop(0, steps, extra, 0)
-    else:
-        lax.fori_loop(0, copies, send_one, 0)
-        lax.fori_loop(0, slots * steps, own_piece, 0)
+    lax.fori_loop(0, jobs, run, 0)
 
     lane = lax.broadcasted_iota(jnp.int32, (LAGS, 2 * LAGS), 1)
     lag = lane % LAGS
-    away = jnp.abs(lag - HALF)
-    half = lane - lag
-    even_at = half + away
-    odd_at = half + HALF + jnp.minimum(away, HALF - 1)
-    sign = jnp.where(lag > HALF, 1.0, jnp.where((lag > 0) & (lag < HALF), -1.0, 0.0))
+    order = lane - lag + jnp.where(lag < HALF, lax.rem(HALF - lag, HALF), lag)
+    first_row = lax.broadcasted_iota(jnp.int32, (HALF, channels), 0) == 0
+
+    def halves(x):
+        even, odd = x[:HALF], x[HALF:]
+        return [
+            jnp.where(first_row, odd, even - odd), even + jnp.where(first_row, 0.0, odd)
+        ]
 
     def joined(x):
-        even = jnp.take_along_axis(x, even_at, axis=1)
-        odd = jnp.take_along_axis(x, odd_at, axis=1)
-        return even + sign * odd
+        return jnp.take_along_axis(x, order, axis=1)
 
     def finish(n, carry):
         slot, step = n // steps, lax.rem(n, steps)
@@ -322,7 +333,10 @@
         for f in finals:
             total = total + recv[f, slot, span(step), :].astype(jnp.float32)
         for q in range(GROUP // 2):
-            turned[q] = total[q * 2 * LAGS : (q + 1) * 2 * LAGS].T
+            start = q * 2 * LAGS
+            both = halves(total[start : start + LAGS])
+            both += halves(total[start + LAGS : start + 2 * LAGS])
+            turned[q] = jnp.concatenate(both, 0).T
         for q in range(GROUP // 2):
             first = turned[q, pl.ds(0, LAGS, stride=2), :]
             second = turned[q, pl.ds(1, LAGS, stride=2), :]

time: 110 us -> 109 us (level)
  no operation moved by 1% of the time
where the time goes in v5:
time: 109 us
  Pallas kernels  101 us (93%)
  local copies, waits for them, and re-layouts  5.4 us (5%)
  other arithmetic  1.69 us (2%)
    pallas_call x1, Pallas kernels, stacked(): pl.pallas_call(functools.partial(stack_kernel, days, owners, width, used)...  101 us
    unnamed x7, local copies, waits for them, and re-layouts  2.77 us
    gather x3, local copies, waits for them, and re-layouts, per_device(): moved = jnp.take(local, picks, axis=1).reshape(channels, used * 2 * width)  2.52 us

profile of v5, /device:TPU:11, one launch (start us, length us, event | category | flops | bytes accessed | tf_op | source)
XLA Modules:
  0.0 109.3 jit_solution(3890204154399896623)
XLA Ops:
  0.0 0.0 copy-start.2
  0.0 2.8 %copy.9 = bf16[1,128,4,2048]{3,1,2,0:T(8,128)(2,1)S(1)} copy(bf16[1,128,4,2048]{3,2,1,0:T(4,128)(2,1)} %param.5) | data formatting | bytes 4194304 | tf_op args[0]
  2.8 0.0 copy-done.2
  2.8 0.6 gather_fusion
  3.4 1.1 copy.7
  4.5 0.0 copy-start.1
  4.5 0.0 copy-start
  4.5 0.8 gather.7
  5.4 0.1 broadcast_in_dim.27
  5.5 0.1 broadcast_select_fusion.1.near_ref
  5.6 0.0 copy-done.1
  5.6 0.0 copy-done
  5.6 101.5 %shard_map.55 = f32[2,32,8192]{2,1,0:T(8,128)S(1)} custom-call(bf16[1,128,4096]{2,1,0:T(8,128)(2,1)S(1)} %broadcast_select_fusion.1.near_ref, s32[2,2]{1,0:T(2,128)S(1)} %xor_bitcast_fusion.place_ref, bf16[80,1024]{1,0:T(8,128)(2,1)S(1)} %copy-done), custom_call_target="tpu_custom_call" | custom-call | flops 17179869184 | bytes 8388608 | tf_op jit(solution)/shard_map/pallas_call | solution.py:388
  107.8 1.5 %broadcast_select_fusion = f32[2,32,8192]{2,1,0:T(8,128)} fusion(f32[2,32,8192]{2,1,0:T(8,128)S(1)} %shard_map.55, pred[2]{0:T(512)(128)(4,1)S(1)} %iota_compare_fusion), kind=kLoop, calls=%fused_computation.2 | loop fusion | flops 524288 | bytes 4194306 | tf_op jit(solution)/shard_map/jit(_where)/select_n | solution.py:450
  (6 shorter events, 0.1 us)
Async XLA Ops:
  0.0 2.8 %copy-start.2 = (s32[1,2]{1,0:T(1,128)S(1)}, s32[1,2]{1,0:T(1,128)}, u32[]{:S(2)}) copy-start(s32[1,2]{1,0:T(1,128)} %param.6) | copy-start | bytes 28
  4.5 1.1 %copy-start.1 = (s32[1,2,2]{2,1,0:T(2,128)S(1)}, s32[1,2,2]{2,1,0:T(2,128)}, u32[]{:S(2)}) copy-start(s32[1,2,2]{2,1,0:T(2,128)} %param.7) | copy-start | bytes 52
  4.5 1.1 %copy-start = (bf16[80,1024]{1,0:T(8,128)(2,1)S(1)}, bf16[80,1024]{1,0:T(8,128)(2,1)}, u32[]{:S(2)}) copy-start(bf16[80,1024]{1,0:T(8,128)(2,1)} %constant.25.clone.rows_ref) | copy-start | bytes 491524
